TPU v7x, 32 devices: a whole 2x2x4 slice. The times are simulated.
32 devices in a mesh: cell: 8 (over z, y), view: 4 (over x, core).
Axes of the slice: x: 2, y: 2, z: 4, core: 2. Of those that a mesh axis runs over, the one named last changes fastest.
Arguments:
- gaussians: float32 [128, 9, 256], P('cell'), as said below
- seg_count: int32 [4, 8], P('view', 'cell'), may hold values from 1 to 3, as said below
- seg_block: int32 [4, 8, 3], P('view', 'cell'), may hold values from 0 to 127, as said below
- ray_count: int32 [4, 8], P('view', 'cell'), may hold values from 576 to 2304
- camera_shift: float32 [4, 2], P('view'), may hold values from -6 to 6
- target: float32 [4, 8, 3, 2304], P('view', 'cell'), may hold values from 0 to 1
Outputs:
- image: float32 [4, 8, 3, 2304], P('view', 'cell')
- gauss_grad: float32 [128, 9, 256], P('cell')
Inputs may be any that keep to these rules, and one draw needn't show every extreme that they name: `gaussians`: each column of a block is one Gaussian: a mean, the entries a, b, c of a positive definite inverse covariance, an opacity in (0, 1), three colours. `seg_count`: tiles 2m and 2m + 1 of a view hold 4 segments together; in every view some tile holds 3. Segment k of tile t uses a block stored in cell seg_block // 16, which is t + e modulo 8 for some e from -2 to 2; entries at k >= seg_count are not used.
All inputs are finite; a program needn't handle non-finite values.
Results may differ from a plain program's by a relative error of at most 0.0003.
Values sent between devices are 32-bit elements; how exact they have to be, the bound alone decides.
A program may use at most 64 MiB of HBM per device.

v0:
```python
import functools

import jax
import jax.numpy as jnp
from jax import lax
from jax.experimental import pallas as pl
from jax.experimental.pallas import tpu as pltpu
from jax.sharding import PartitionSpec as P

TILE = 48
LANES = 128
LOG2E = 1.4426950408889634
MESH = pl.DeviceIdType.MESH
F32 = jnp.float32
BF16 = jnp.bfloat16


def split(value):
    high = value.astype(BF16)
    return high, (value - high.astype(F32)).astype(BF16)


def dot(left, right):
    return jnp.dot(left, right, preferred_element_type=F32)


def dot_nt(left, right):
    return lax.dot_general(left, right, (((1,), (1,)), ((), ())), preferred_element_type=F32)


def cell_peers(cells, me):
    side = me % 2
    base = me - side
    peers = [((base + 1 - side) % cells, 0, 3 - side, 2 + side)]
    for pair in (-1, 1):
        for other in (0, 1):
            cell = (base + 2 * pair + other + cells) % cells
            peers.append((cell, pair, 2 * pair + 2 + other, side + 2 - 2 * pair))
    return peers


def pair_ids(even, odd, slots):
    count = even[0:1, 0:1]
    ids = []
    for s in range(slots + 1):
        picked = even[0:1, 1 + min(s, slots - 1) : 2 + min(s, slots - 1)]
        for k in range(slots):
            picked = jnp.where(count == s - k, odd[0:1, 1 + k : 2 + k], picked)
        ids.append(picked)
    return ids


def over(value, divisor):
    return jnp.floor((value + 0.5) * (1.0 / divisor))


def iota(shape, axis):
    return lax.broadcasted_iota(jnp.int32, shape, axis).astype(F32)


def round_up(value, unit):
    return -(-value // unit) * unit


def step_kernel(
    cells, views, slots, rows, chunk, sub,
    count_ref, block_ref, ray_ref, shift_ref, gauss_in, tgt_in, out_ref, out_img,
    gauss_ref, gauss_parts, tgt_ref, tgts, info, infos, half_out, resp, got, par_ref, grad_ref, got_grad,
    img_out, img_in, part, quarter, full, alphas, weights, w_pair, stage, h_pair, moments, cgrads,
    load_sem, info_send, info_recv, tgt_send, tgt_recv, blk_send, blk_recv,
    img_send, img_recv, seg_send, seg_recv, part_send, part_recv, full_send, full_recv,
):
    me = lax.axis_index("cell")
    view = lax.axis_index("view")
    side = me % 2
    segs = slots + 1
    dense_rows, size = gauss_ref.shape
    per_block = dense_rows // rows
    pack = par_ref.shape[0]
    half = tgts.shape[2]
    channels = tgt_ref.shape[0]
    peers = cell_peers(cells, me)
    others = [(view + k) % views for k in range(1, views)]

    def to_cell(src, dst, send, recv, cell):
        return pltpu.make_async_remote_copy(
            src, dst, send, recv, device_id={"cell": cell}, device_id_type=MESH
        )

    def to_view(src, dst, send, recv, other):
        return pltpu.make_async_remote_copy(
            src, dst, send, recv, device_id={"view": other}, device_id_type=MESH
        )

    gauss_load = pltpu.make_async_copy(gauss_in, gauss_ref, load_sem.at[0])
    gauss_load.start()
    tgt_load = pltpu.make_async_copy(tgt_in, tgt_ref, load_sem.at[1])
    tgt_load.start()
    barrier = pltpu.get_barrier_semaphore()
    for cell, _, _, _ in peers:
        pl.semaphore_signal(barrier, inc=1, device_id={"cell": cell}, device_id_type=MESH)
    for other in others:
        pl.semaphore_signal(barrier, inc=1, device_id={"view": other}, device_id_type=MESH)
    lane = lax.broadcasted_iota(jnp.int32, info.shape, 1)
    fields = jnp.where(lane == 0, count_ref[0, 0], 0)
    for s in range(slots):
        fields = jnp.where(lane == 1 + s, block_ref[0, 0, s], fields)
    fields = jnp.where(lane == 1 + slots, ray_ref[0, 0], fields)
    info[...] = fields
    infos[2 + side] = fields
    gauss_load.wait()
    gauss = gauss_ref[...]
    high = gauss.astype(BF16)
    rest = gauss - high.astype(F32)
    middle = rest.astype(BF16)
    gauss_parts[:dense_rows] = high
    gauss_parts[dense_rows : 2 * dense_rows] = middle
    gauss_parts[2 * dense_rows : 3 * dense_rows] = (rest - middle.astype(F32)).astype(BF16)
    spare = gauss_parts.shape[0] - 3 * dense_rows
    if spare:
        gauss_parts[3 * dense_rows :] = jnp.zeros((spare, size), BF16)
    tgt_load.wait()
    blank = jnp.zeros((8 - channels, half), F32)

    def tile_half(which):
        cols = pl.ds(pl.multiple_of(which * half, LANES), half)
        return jnp.concatenate([tgt_ref[r, :, cols] for r in range(channels)] + [blank], axis=0)

    half_out[...] = tile_half(1 - side)
    tgts[side] = tile_half(side)
    moments[...] = jnp.zeros_like(moments)
    cgrads[...] = jnp.zeros_like(cgrads)
    pl.semaphore_wait(barrier, len(peers) + len(others))

    sends = []
    for n, (cell, _, _, theirs) in reversed(list(enumerate(peers))):
        sends.append(to_cell(info, infos.at[theirs], info_send.at[n], info_recv.at[theirs], cell))
        sends[-1].start()
    tgt_copy = to_cell(half_out, tgts.at[side], tgt_send, tgt_recv, peers[0][0])
    tgt_copy.start()

    row_id = iota((pack, gauss_parts.shape[0]), 0)
    row_param = over(row_id, segs)
    row_slot = row_id - segs * row_param
    lane_id = iota((pack, gauss_parts.shape[0]), 1)
    lane_part = over(lane_id, dense_rows)
    lane_id = lane_id - dense_rows * lane_part
    lane_param = over(lane_id, per_block)
    same = (row_param == lane_param) & (lane_part < 3.0)
    lane_block = lane_id - per_block * lane_param
    local = {}
    for pair in (-1, 1, 0):
        for n, (cell, distance, mine, _) in enumerate(peers):
            if distance == pair:
                to_cell(info, infos.at[mine], info_send.at[n], info_recv.at[mine], cell).wait_recv()
        ids = pair_ids(infos[2 * pair + 2], infos[2 * pair + 3], slots)
        local[pair] = [(block - me * per_block).astype(F32) for block in ids]
        wanted = jnp.full(row_id.shape, -1.0, F32)
        for s in range(segs):
            wanted = jnp.where(row_slot == float(s), local[pair][s], wanted)
        chosen = jnp.where(same & (lane_block == wanted), 1.0, 0.0).astype(BF16)
        resp[pair + 1] = dot(chosen, gauss_parts[...])
        for n, (cell, distance, _, theirs) in enumerate(peers):
            if distance == pair:
                sends.append(to_cell(resp.at[pair + 1], got.at[theirs], blk_send.at[n], blk_recv.at[theirs], cell))
                sends[-1].start()

    even, odd = infos[2], infos[3]
    count, ray_even, ray_odd = even[0:1, 0:1], even[0:1, slots + 1 : slots + 2], odd[0:1, slots + 1 : slots + 2]
    shift_x, shift_y = shift_ref[0:1, 0:1], shift_ref[0:1, 1:2]
    centre = (TILE - 1) / 2.0
    row_ids = lax.broadcasted_iota(jnp.int32, (size, size), 0)
    col_ids = lax.broadcasted_iota(jnp.int32, (size, size), 1)
    before = (row_ids < col_ids).astype(F32).astype(BF16)
    after = (row_ids > col_ids).astype(F32).astype(BF16)
    before = jnp.concatenate([before, before], axis=0)
    after = jnp.concatenate([after, after], axis=0)
    parts = [slice(r, r + sub) for r in range(0, chunk, sub)]
    whole = slice(0, chunk)
    dense_row = iota((dense_rows, round_up(3 * pack, LANES)), 0)
    dense_param = over(dense_row, per_block)
    dense_block = dense_row - per_block * dense_param
    pack_lane = iota(dense_row.shape, 1)
    pack_pair = over(pack_lane, pack)
    pack_lane = pack_lane - pack * pack_pair
    pack_param = over(pack_lane, segs)
    pack_slot = pack_lane - segs * pack_param
    wanted = jnp.full(dense_row.shape, -1.0, F32)
    for pair in (-1, 0, 1):
        for s in range(segs):
            here = (pack_pair == float(pair + 1)) & (pack_slot == float(s))
            wanted = jnp.where(here, local[pair][s], wanted)
    placing = jnp.where((dense_param == pack_param) & (dense_block == wanted), 1.0, 0.0).astype(BF16)

    total = resp[1]
    for n, (cell, distance, mine, _) in enumerate(peers):
        to_cell(resp.at[distance + 1], got.at[mine], blk_send.at[n], blk_recv.at[mine], cell).wait_recv()
        total = total + got[mine]
    par_ref[...] = total
    tgt_copy.wait_recv()

    def param(s, r):
        return par_ref[r * segs + s : r * segs + s + 1]

    def place(ids):
        ids = ids.astype(F32)
        row = over(ids, TILE)
        return ids - TILE * row - centre, row - centre

    def at(s, rows):
        return slice(s * chunk + rows.start, s * chunk + rows.stop)

    image_rows, shade_rows = [], []
    for s in range(segs):
        colours = jnp.concatenate([param(s, 6 + r) for r in range(3)] + [jnp.zeros((5, size), F32)], axis=0)
        in_even = (count > s).astype(F32)
        both = jnp.concatenate([colours * in_even, colours * (1.0 - in_even)], axis=0)
        c_hi = both.astype(BF16).astype(F32)
        c_lo = both - c_hi
        pieces = jnp.concatenate([c_hi, c_lo], axis=0).astype(BF16)
        image_rows.append(jnp.concatenate([pieces, pieces], axis=1))
        shade_rows.append(
            jnp.concatenate([c_hi, c_hi, c_lo, jnp.zeros((LANES - 48, size), F32)], axis=0).astype(BF16)
        )
    shade_rows = jnp.concatenate(shade_rows, axis=1)

    def steps(c):
        cols = slice(c * chunk, (c + 1) * chunk)
        first = side * half + c * chunk
        for rows in parts:
            x_0, y_0 = place(first + rows.start + lax.broadcasted_iota(jnp.int32, (sub, size), 0))
            x_0, y_0 = x_0 - shift_x, y_0 - shift_y
            for s in range(segs):
                row = functools.partial(param, s)
                dx = x_0 - row(0)
                dy = y_0 - row(1)
                power = dx * ((-0.5 * LOG2E) * row(2) * dx + (-LOG2E) * row(3) * dy)
                alpha = row(5) * jnp.exp2(power + ((-0.5 * LOG2E) * row(4) * dy) * dy)
                alphas[c, at(s, rows)] = alpha
                high, low = split(jnp.log(1.0 - alpha))
                stage[c, at(s, rows), :size] = high
                stage[c, at(s, rows), size:] = low
        yield
        prefix = dot(stage[c], before)
        yield
        for rows in parts:
            carry = jnp.ones((sub, 1), F32)
            for s in range(segs):
                alpha = alphas[c, at(s, rows)]
                trans = jnp.exp(prefix[at(s, rows)]) * carry
                weight = alpha * trans
                weights[c, at(s, rows)] = weight
                high, low = split(weight)
                w_pair[c, at(s, rows), :size] = high
                w_pair[c, at(s, rows), size:] = low
                carry = jnp.where(count == s + 1, 1.0, (trans - weight)[:, size - 1 :])
        yield
        image = jnp.zeros((32, chunk), F32)
        for s in range(segs):
            image = image + dot_nt(image_rows[s], w_pair[c, at(s, whole)])
        yield
        in_tile = lax.broadcasted_iota(jnp.int32, (16, chunk), 0) < 8
        lane_ids = first + lax.broadcasted_iota(jnp.int32, (16, chunk), 1)
        live = (lane_ids < jnp.where(in_tile, ray_even, ray_odd)).astype(F32)
        rendered = (image[:16] + image[16:]) * live
        own = jnp.where(side == 0, rendered[:8], rendered[8:])
        img_out[:, cols] = jnp.where(side == 0, rendered[8:], rendered[:8])
        for r in range(channels):
            out_img[r, :, pl.ds(pl.multiple_of(first, LANES), chunk)] = own[r : r + 1]
        target = jnp.concatenate([tgts[0, :, cols], tgts[1, :, cols]], axis=0)
        residual = (rendered - target) * live
        r_hi = residual.astype(BF16).astype(F32)
        r_lo = residual - r_hi
        spread = jnp.concatenate([r_hi, r_lo, r_hi, jnp.zeros((LANES - 48, chunk), F32)], axis=0)
        spread = jnp.transpose(spread).astype(BF16)
        r_rows = jnp.concatenate([r_hi, r_lo], axis=0).astype(BF16)
        x_l, y_l = place(lane_ids[:1])
        squares = [x_l * x_l, x_l * y_l, y_l * y_l]
        sq_hi = [q.astype(BF16).astype(F32) for q in squares]
        none = jnp.zeros_like(x_l)
        features = [none + 1.0, x_l, y_l] + sq_hi + [none] * 5 + [q - h for q, h in zip(squares, sq_hi)] + [none] * 2
        features = jnp.concatenate(features, axis=0).astype(BF16)
        features = jnp.concatenate([features, features], axis=1)
        shaded = dot(spread, shade_rows)
        yield
        for rows in parts:
            for s in range(segs):
                product = weights[c, at(s, rows)] * shaded[rows, s * size : (s + 1) * size]
                weights[c, at(s, rows)] = product
                high, low = split(product)
                stage[c, at(s, rows), :size] = high
                stage[c, at(s, rows), size:] = low
        yield
        later = dot(stage[c], after)
        for s in range(segs):
            cgrads[s] += dot(r_rows, w_pair[c, at(s, whole)])
        yield
        for rows in parts:
            carry = jnp.zeros((sub, 1), F32)
            for s in reversed(range(segs)):
                product = weights[c, at(s, rows)]
                alpha = alphas[c, at(s, rows)]
                tail = later[at(s, rows)] + carry
                carry = jnp.where(count == s, 0.0, (tail + product)[:, :1])
                rest = 1.0 - alpha
                inverse = pl.reciprocal(rest, approx=True)
                inverse = inverse * (2.0 - rest * inverse)
                high, low = split(product - alpha * inverse * tail)
                h_pair[c, s, rows] = high
                h_pair[c, s, slice(chunk + rows.start, chunk + rows.stop)] = low
        yield
        for s in range(segs):
            moments[s] += dot(features, h_pair[c, s])
        yield

    chunks = [steps(c) for c in range(half // chunk)]
    for tick in range(9 + len(chunks) - 1):
        for c, stages in enumerate(chunks):
            if 0 <= tick - c < 9:
                next(stages)

    img_copy = to_cell(img_out, img_in, img_send, img_recv, peers[0][0])
    img_copy.start()
    grad_ref[...] = jnp.zeros_like(grad_ref)
    for s in range(segs):
        row = functools.partial(param, s)
        mean_x, mean_y = row(0) + shift_x, row(1) + shift_y
        m = [moments[s, k : k + 1] for k in range(3)] + [
            moments[s, k : k + 1] + moments[s, k + 8 : k + 9] for k in range(3, 6)
        ]
        along_x = m[1] - mean_x * m[0]
        along_y = m[2] - mean_y * m[0]
        square_x = m[3] - 2.0 * mean_x * m[1] + mean_x * mean_x * m[0]
        cross_xy = m[4] - mean_x * m[2] - mean_y * m[1] + mean_x * mean_y * m[0]
        square_y = m[5] - 2.0 * mean_y * m[2] + mean_y * mean_y * m[0]
        cg = cgrads[s, :16] + cgrads[s, 16:]
        cg = cg[:, :size] + cg[:, size:]
        grads = [
            row(2) * along_x + row(3) * along_y,
            row(3) * along_x + row(4) * along_y,
            -0.5 * square_x,
            -cross_xy,
            -0.5 * square_y,
            m[0] / row(5),
            jnp.where(count > s, cg[0:3], cg[8:11]),
        ]
        for r, value in enumerate(grads[:6] + [grads[6][k : k + 1] for k in range(3)]):
            grad_ref[r * segs + s : r * segs + s + 1] = value

    for n, (cell, _, _, theirs) in reversed(list(enumerate(peers))):
        sends.append(to_cell(grad_ref, got_grad.at[theirs], seg_send.at[n], seg_recv.at[theirs], cell))
        sends[-1].start()
    sums = {}
    for pair in (0, -1, 1):
        for n, (cell, distance, mine, _) in enumerate(peers):
            if distance == pair:
                to_cell(grad_ref, got_grad.at[mine], seg_send.at[n], seg_recv.at[mine], cell).wait_recv()
        if pair == 0:
            sums[pair] = grad_ref[...] + got_grad[3 - side]
        else:
            sums[pair] = got_grad[2 * pair + 2] + got_grad[2 * pair + 3]
    spare = placing.shape[1] - 3 * pack
    stacked = [sums[-1], sums[0], sums[1]] + ([jnp.zeros((spare, size), F32)] if spare else [])
    high, low = split(jnp.concatenate(stacked, axis=0))
    dense = dot(placing, high) + dot(placing, low)
    part[:dense_rows] = dense[:, : size // 2]
    part[dense_rows:] = dense[:, size // 2 :]

    share = part.shape[0] // views

    def share_of(which):
        return pl.ds(pl.multiple_of(which * share, 8), share)

    part_copies = []
    for k, other in enumerate(others):
        part_copies.append(to_view(part.at[share_of(other)], quarter.at[k], part_send.at[k], part_recv.at[k], other))
        part_copies[-1].start()
    total = part[share_of(view)]
    for k, copy in enumerate(part_copies):
        copy.wait_recv()
        total = total + quarter[k]
    full[share_of(view)] = total
    for k, other in enumerate(others):
        mine = full.at[share_of(view)]
        sends.append(to_view(mine, mine, full_send.at[k], full_recv.at[k], other))
        sends[-1].start()
    img_copy.wait_recv()
    for r in range(channels):
        out_img[r, :, pl.ds(pl.multiple_of((1 - side) * half, LANES), half)] = img_in[r : r + 1]
    for k in range(views - 1):
        theirs = full.at[share_of((view + views - 1 - k) % views)]
        to_view(theirs, theirs, full_send.at[k], full_recv.at[k], others[k]).wait_recv()
    out_ref[:, : size // 2] = full[:dense_rows]
    out_ref[:, size // 2 :] = full[dense_rows:]
    for copy in sends + part_copies + [tgt_copy, img_copy]:
        copy.wait_send()


def step(cells, views, seg_count, seg_block, ray_count, shift, gaussians, target, rows):
    slots = seg_block.shape[2]
    segs = slots + 1
    dense_rows, size = gaussians.shape
    half = target.shape[2] // 2
    chunk = next(c for c in (384, 256, 128) if half % c == 0)
    count = half // chunk
    pack = (round_up(rows * segs, 8), size)
    share = 2 * dense_rows // views
    vmem = pl.BlockSpec(memory_space=pltpu.VMEM)
    smem = pl.BlockSpec(memory_space=pltpu.SMEM)
    hbm = pl.BlockSpec(memory_space=pl.ANY)
    dma = pltpu.SemaphoreType.DMA
    return pl.pallas_call(
        functools.partial(step_kernel, cells, views, slots, rows, chunk, chunk),
        out_shape=(
            jax.ShapeDtypeStruct(gaussians.shape, F32),
            jax.ShapeDtypeStruct(target.shape, F32),
        ),
        in_specs=[smem] * 3 + [vmem] + [hbm] * 2,
        out_specs=(vmem,) * 2,
        scratch_shapes=[
            pltpu.VMEM(gaussians.shape, F32),
            pltpu.VMEM((round_up(3 * dense_rows, LANES), size), BF16),
            pltpu.VMEM(target.shape, F32),
            pltpu.VMEM((2, 8, half), F32),
            pltpu.VMEM((8, LANES), jnp.int32),
            pltpu.VMEM((6, 8, LANES), jnp.int32),
            pltpu.VMEM((8, half), F32),
            pltpu.VMEM((3,) + pack, F32),
            pltpu.VMEM((6,) + pack, F32),
            pltpu.VMEM(pack, F32),
            pltpu.VMEM(pack, F32),
            pltpu.VMEM((6,) + pack, F32),
            pltpu.VMEM((8, half), F32),
            pltpu.VMEM((8, half), F32),
            pltpu.VMEM((2 * dense_rows, size // 2), F32),
            pltpu.VMEM((views - 1, share, size // 2), F32),
            pltpu.VMEM((2 * dense_rows, size // 2), F32),
            pltpu.VMEM((count, segs * chunk, size), F32),
            pltpu.VMEM((count, segs * chunk, size), F32),
            pltpu.VMEM((count, segs * chunk, 2 * size), BF16),
            pltpu.VMEM((count, segs * chunk, 2 * size), BF16),
            pltpu.VMEM((count, segs, 2 * chunk, size), BF16),
            pltpu.VMEM((segs, 16, size), F32),
            pltpu.VMEM((segs, 32, 2 * size), F32),
            dma((2,)), dma((5,)), dma((6,)), dma, dma, dma((5,)), dma((6,)),
            dma, dma, dma((5,)), dma((6,)),
            dma((views - 1,)), dma((views - 1,)), dma((views - 1,)), dma((views - 1,)),
        ],
        compiler_params=pltpu.CompilerParams(
            collective_id=0, has_side_effects=True, vmem_limit_bytes=54 * 2**20
        ),
        name="splat_step",
    )(seg_count, seg_block, ray_count, shift, gaussians, target)


def shards(cells, views, gaussians, seg_count, seg_block, ray_count, camera_shift, target):
    blocks, rows, size = gaussians.shape
    by_row = gaussians.transpose(1, 0, 2).reshape(rows * blocks, size)
    planes = target.reshape(target.shape[2], 1, target.shape[3])
    grads, image = step(cells, views, seg_count, seg_block, ray_count, camera_shift, by_row, planes, rows)
    return (image.reshape(target.shape), grads.reshape(rows, blocks, size).transpose(1, 0, 2))


def solution(mesh):
    placed = (
        P("cell", None, None),
        P("view", "cell"),
        P("view", "cell", None),
        P("view", "cell"),
        P("view", None),
        P("view", "cell", None, None),
    )
    return jax.shard_map(
        functools.partial(shards, mesh.shape["cell"], mesh.shape["view"]),
        mesh=mesh,
        in_specs=placed,
        out_specs=(P("view", "cell", None, None), P("cell", None, None)),
        check_vma=False,
    )
```

profile of v0, /device:TPU:0, one launch (start us, length us, event | category | flops | bytes accessed | tf_op | source)
XLA Modules:
  0.0 42.7 jit_solution(13685904707090289812)
XLA Ops:
  1.9 37.8 %splat_step.1 = (f32[144,256]{1,0:T(8,128)}, f32[3,1,2304]{2,1,0:T(1,128)}) custom-call(s32[1,1]{1,0:T(1,128)S(6)} %copy.11.count_ref, s32[1,1,3]{2,1,0:T(1,128)} %block_ref.1, s32[1,1]{1,0:T(1,128)S(6)} %copy.12.ray_ref, f32[1,2]{1,0:T(1,128)} %shift_ref.1, f32[144,256]{1,0:T(8,128)} %bitcast.10, f32[3,1,2304]{2,1,0:T(1,128)} %bitcast.13), custom_call_target="tpu_custom_call" | custom-call | tf_op jit(solution)/shard_map/splat_step/pallas_call | solution.py:412
  39.8 1.4 %copy.13 = f32[1,1,3,2304]{3,1,2,0:T(1,128)} copy(f32[1,1,3,2304]{3,1,2,0:T(1,128)} %bitcast.12) | data formatting | bytes 55296
  41.1 1.6 %copy.14 = f32[16,9,256]{2,0,1:T(8,128)} copy(f32[16,9,256]{2,0,1:T(8,128)} %bitcast.11) | data formatting | bytes 294912
where the time goes:
time: 42.9 us; the launch traced here: 42.7 us
  Pallas kernels  37.8 us (88%)
  local copies, waits for them, and re-layouts  2.94 us (7%)
  between operations  1.93 us (4%)
    pallas_call x1, Pallas kernels, step(): pl.pallas_call(functools.partial(step_kernel, cells, views, slots, rows,...  37.8 us
    unnamed x2, local copies, waits for them, and re-layouts  2.94 us

commit v1 on v0

--- a/solution.py
+++ b/solution.py
@@ -64,9 +64,9 @@
 
 def step_kernel(
     cells, views, slots, rows, chunk, sub,
-    count_ref, block_ref, ray_ref, shift_ref, gauss_in, tgt_in, out_ref, out_img,
+    count_ref, block_ref, ray_ref, shift_ref, gauss_in, tgt_in, full, out_img,
     gauss_ref, gauss_parts, tgt_ref, tgts, info, infos, half_out, resp, got, par_ref, grad_ref, got_grad,
-    img_out, img_in, part, quarter, full, alphas, weights, w_pair, stage, h_pair, moments, cgrads,
+    img_out, img_in, part, quarter, alphas, weights, w_pair, stage, h_pair, moments, cgrads, flat_x, delta_x, cross_y, flat_y,
     load_sem, info_send, info_recv, tgt_send, tgt_recv, blk_send, blk_recv,
     img_send, img_recv, seg_send, seg_recv, part_send, part_recv, full_send, full_recv,
 ):
@@ -223,19 +223,25 @@
             jnp.concatenate([c_hi, c_hi, c_lo, jnp.zeros((LANES - 48, size), F32)], axis=0).astype(BF16)
         )
     shade_rows = jnp.concatenate(shade_rows, axis=1)
+    x_0 = iota((TILE, size), 0) - centre - shift_x
+    y_0 = iota(flat_y.shape[1:], 0) + (side * (half // TILE)).astype(F32) - centre - shift_y
+    for s in range(segs):
+        dx = x_0 - param(s, 0)
+        dy = y_0 - param(s, 1)
+        delta_x[s] = dx
+        flat_x[s] = ((-0.5 * LOG2E) * param(s, 2)) * dx * dx + LOG2E * jnp.log(param(s, 5))
+        cross_y[s] = (-LOG2E) * param(s, 3) * dy
+        flat_y[s] = ((-0.5 * LOG2E) * param(s, 4)) * dy * dy
 
     def steps(c):
         cols = slice(c * chunk, (c + 1) * chunk)
         first = side * half + c * chunk
-        for rows in parts:
-            x_0, y_0 = place(first + rows.start + lax.broadcasted_iota(jnp.int32, (sub, size), 0))
-            x_0, y_0 = x_0 - shift_x, y_0 - shift_y
-            for s in range(segs):
-                row = functools.partial(param, s)
-                dx = x_0 - row(0)
-                dy = y_0 - row(1)
-                power = dx * ((-0.5 * LOG2E) * row(2) * dx + (-LOG2E) * row(3) * dy)
-                alpha = row(5) * jnp.exp2(power + ((-0.5 * LOG2E) * row(4) * dy) * dy)
+        for s in range(segs):
+            for k in range(chunk // TILE):
+                rows = slice(k * TILE, (k + 1) * TILE)
+                r = c * (chunk // TILE) + k
+                power = flat_x[s] + delta_x[s] * cross_y[s, r : r + 1] + flat_y[s, r : r + 1]
+                alpha = jnp.exp2(power)
                 alphas[c, at(s, rows)] = alpha
                 high, low = split(jnp.log(1.0 - alpha))
                 stage[c, at(s, rows), :size] = high
@@ -390,8 +396,6 @@
     for k in range(views - 1):
         theirs = full.at[share_of((view + views - 1 - k) % views)]
         to_view(theirs, theirs, full_send.at[k], full_recv.at[k], others[k]).wait_recv()
-    out_ref[:, : size // 2] = full[:dense_rows]
-    out_ref[:, size // 2 :] = full[dense_rows:]
     for copy in sends + part_copies + [tgt_copy, img_copy]:
         copy.wait_send()
 
@@ -401,7 +405,7 @@
     segs = slots + 1
     dense_rows, size = gaussians.shape
     half = target.shape[2] // 2
-    chunk = next(c for c in (384, 256, 128) if half % c == 0)
+    chunk = next(c for c in (384, half) if half % c == 0)
     count = half // chunk
     pack = (round_up(rows * segs, 8), size)
     share = 2 * dense_rows // views
@@ -412,7 +416,7 @@
     return pl.pallas_call(
         functools.partial(step_kernel, cells, views, slots, rows, chunk, chunk),
         out_shape=(
-            jax.ShapeDtypeStruct(gaussians.shape, F32),
+            jax.ShapeDtypeStruct((2 * dense_rows, size // 2), F32),
             jax.ShapeDtypeStruct(target.shape, F32),
         ),
         in_specs=[smem] * 3 + [vmem] + [hbm] * 2,
@@ -434,7 +438,6 @@
             pltpu.VMEM((8, half), F32),
             pltpu.VMEM((2 * dense_rows, size // 2), F32),
             pltpu.VMEM((views - 1, share, size // 2), F32),
-            pltpu.VMEM((2 * dense_rows, size // 2), F32),
             pltpu.VMEM((count, segs * chunk, size), F32),
             pltpu.VMEM((count, segs * chunk, size), F32),
             pltpu.VMEM((count, segs * chunk, 2 * size), BF16),
@@ -442,6 +445,10 @@
             pltpu.VMEM((count, segs, 2 * chunk, size), BF16),
             pltpu.VMEM((segs, 16, size), F32),
             pltpu.VMEM((segs, 32, 2 * size), F32),
+            pltpu.VMEM((segs, TILE, size), F32),
+            pltpu.VMEM((segs, TILE, size), F32),
+            pltpu.VMEM((segs, half // TILE, size), F32),
+            pltpu.VMEM((segs, half // TILE, size), F32),
             dma((2,)), dma((5,)), dma((6,)), dma, dma, dma((5,)), dma((6,)),
             dma, dma, dma((5,)), dma((6,)),
             dma((views - 1,)), dma((views - 1,)), dma((views - 1,)), dma((views - 1,)),
@@ -453,11 +460,40 @@
     )(seg_count, seg_block, ray_count, shift, gaussians, target)
 
 
+def finish_kernel(full, image, out_ref, out_img, sems):
+    rows, size = out_ref.shape
+    copies = [pltpu.make_async_copy(image, out_img, sems.at[0])]
+    for h in range(2):
+        lanes = out_ref.at[:, h * (size // 2) : (h + 1) * (size // 2)]
+        copies.append(pltpu.make_async_copy(full.at[h * rows : (h + 1) * rows], lanes, sems.at[1 + h]))
+    for copy in copies:
+        copy.start()
+    for copy in copies:
+        copy.wait()
+
+
+def finish(full, image):
+    anywhere = pl.BlockSpec(memory_space=pl.ANY)
+    return pl.pallas_call(
+        finish_kernel,
+        out_shape=(
+            jax.ShapeDtypeStruct((full.shape[0] // 2, 2 * full.shape[1]), F32),
+            jax.ShapeDtypeStruct(image.shape, F32),
+        ),
+        in_specs=[anywhere] * 2,
+        out_specs=(anywhere,) * 2,
+        scratch_shapes=[pltpu.SemaphoreType.DMA((3,))],
+        compiler_params=pltpu.CompilerParams(vmem_limit_bytes=60 * 2**20),
+        name="place_results",
+    )(full, image)
+
+
 def shards(cells, views, gaussians, seg_count, seg_block, ray_count, camera_shift, target):
     blocks, rows, size = gaussians.shape
     by_row = gaussians.transpose(1, 0, 2).reshape(rows * blocks, size)
     planes = target.reshape(target.shape[2], 1, target.shape[3])
     grads, image = step(cells, views, seg_count, seg_block, ray_count, camera_shift, by_row, planes, rows)
+    grads, image = finish(grads, image)
     return (image.reshape(target.shape), grads.reshape(rows, blocks, size).transpose(1, 0, 2))
 
 

time: 42.9 us -> 45.3 us (1.056)
  Pallas kernels: 37.8 us -> 43.2 us
  local copies, waits for them, and re-layouts: 2.94 us -> 0 us
    pallas_call x0 -> x1, Pallas kernels: none -> 6.43 us  [finish(): pl.pallas_call(finish_kernel, out_shape=(jax.ShapeDtypeStruct((full.shape...]
    unnamed x2 -> x0, local copies, waits for them, and re-layouts: 2.94 us -> none
    pallas_call x1, Pallas kernels: 37.8 us -> 36.8 us  [step(): pl.pallas_call(functools.partial(step_kernel, cells, views, slots, rows,...]
where the time goes in v1:
time: 45.3 us; the launch traced here: 45.1 us
  Pallas kernels  43.2 us (95%)
  between operations  1.93 us (4%)
    pallas_call x1, Pallas kernels, step(): pl.pallas_call(functools.partial(step_kernel, cells, views, slots, rows,...  36.8 us
    pallas_call x1, Pallas kernels, finish(): pl.pallas_call(finish_kernel, out_shape=(jax.ShapeDtypeStruct((full.shape...  6.43 us

profile of v1, /device:TPU:0, one launch (start us, length us, event | category | flops | bytes accessed | tf_op | source)
XLA Modules:
  0.0 45.1 jit_solution(10224727741006311000)
XLA Ops:
  1.9 36.8 %splat_step.1 = (f32[288,128]{1,0:T(8,128)}, f32[3,1,2304]{2,1,0:T(1,128)}) custom-call(s32[1,1]{1,0:T(1,128)S(6)} %copy.9.count_ref, s32[1,1,3]{2,1,0:T(1,128)} %block_ref.1, s32[1,1]{1,0:T(1,128)S(6)} %copy.10.ray_ref, f32[1,2]{1,0:T(1,128)} %shift_ref.1, f32[144,256]{1,0:T(8,128)} %bitcast.10, f32[3,1,2304]{2,1,0:T(1,128)} %bitcast.11), custom_call_target="tpu_custom_call" | custom-call | tf_op jit(solution)/shard_map/splat_step/pallas_call | solution.py:416
  38.7 6.4 %place_results.1 = (f32[144,256]{1,0:T(8,128)}, f32[3,1,2304]{2,1,0:T(1,128)}) custom-call(f32[288,128]{1,0:T(8,128)} %get-tuple-element.6.full, f32[3,1,2304]{2,1,0:T(1,128)} %get-tuple-element.7.image), custom_call_target="tpu_custom_call" | custom-call | tf_op jit(solution)/shard_map/place_results/pallas_call | solution.py:477

commit v2 on v0

--- a/solution.py
+++ b/solution.py
@@ -66,7 +66,7 @@
     cells, views, slots, rows, chunk, sub,
     count_ref, block_ref, ray_ref, shift_ref, gauss_in, tgt_in, out_ref, out_img,
     gauss_ref, gauss_parts, tgt_ref, tgts, info, infos, half_out, resp, got, par_ref, grad_ref, got_grad,
-    img_out, img_in, part, quarter, full, alphas, weights, w_pair, stage, h_pair, moments, cgrads,
+    img_out, img_in, part, quarter, full, alphas, weights, w_pair, stage, h_pair, moments, cgrads, flat_x, delta_x, cross_y, flat_y,
     load_sem, info_send, info_recv, tgt_send, tgt_recv, blk_send, blk_recv,
     img_send, img_recv, seg_send, seg_recv, part_send, part_recv, full_send, full_recv,
 ):
@@ -223,19 +223,25 @@
             jnp.concatenate([c_hi, c_hi, c_lo, jnp.zeros((LANES - 48, size), F32)], axis=0).astype(BF16)
         )
     shade_rows = jnp.concatenate(shade_rows, axis=1)
+    x_0 = iota((TILE, size), 0) - centre - shift_x
+    y_0 = iota(flat_y.shape[1:], 0) + (side * (half // TILE)).astype(F32) - centre - shift_y
+    for s in range(segs):
+        dx = x_0 - param(s, 0)
+        dy = y_0 - param(s, 1)
+        delta_x[s] = dx
+        flat_x[s] = ((-0.5 * LOG2E) * param(s, 2)) * dx * dx + LOG2E * jnp.log(param(s, 5))
+        cross_y[s] = (-LOG2E) * param(s, 3) * dy
+        flat_y[s] = ((-0.5 * LOG2E) * param(s, 4)) * dy * dy
 
     def steps(c):
         cols = slice(c * chunk, (c + 1) * chunk)
         first = side * half + c * chunk
-        for rows in parts:
-            x_0, y_0 = place(first + rows.start + lax.broadcasted_iota(jnp.int32, (sub, size), 0))
-            x_0, y_0 = x_0 - shift_x, y_0 - shift_y
-            for s in range(segs):
-                row = functools.partial(param, s)
-                dx = x_0 - row(0)
-                dy = y_0 - row(1)
-                power = dx * ((-0.5 * LOG2E) * row(2) * dx + (-LOG2E) * row(3) * dy)
-                alpha = row(5) * jnp.exp2(power + ((-0.5 * LOG2E) * row(4) * dy) * dy)
+        for s in range(segs):
+            for k in range(chunk // TILE):
+                rows = slice(k * TILE, (k + 1) * TILE)
+                r = c * (chunk // TILE) + k
+                power = flat_x[s] + delta_x[s] * cross_y[s, r : r + 1] + flat_y[s, r : r + 1]
+                alpha = jnp.exp2(power)
                 alphas[c, at(s, rows)] = alpha
                 high, low = split(jnp.log(1.0 - alpha))
                 stage[c, at(s, rows), :size] = high
@@ -401,7 +407,7 @@
     segs = slots + 1
     dense_rows, size = gaussians.shape
     half = target.shape[2] // 2
-    chunk = next(c for c in (384, 256, 128) if half % c == 0)
+    chunk = next(c for c in (384, half) if half % c == 0)
     count = half // chunk
     pack = (round_up(rows * segs, 8), size)
     share = 2 * dense_rows // views
@@ -442,12 +448,16 @@
             pltpu.VMEM((count, segs, 2 * chunk, size), BF16),
             pltpu.VMEM((segs, 16, size), F32),
             pltpu.VMEM((segs, 32, 2 * size), F32),
+            pltpu.VMEM((segs, TILE, size), F32),
+            pltpu.VMEM((segs, TILE, size), F32),
+            pltpu.VMEM((segs, half // TILE, size), F32),
+            pltpu.VMEM((segs, half // TILE, size), F32),
             dma((2,)), dma((5,)), dma((6,)), dma, dma, dma((5,)), dma((6,)),
             dma, dma, dma((5,)), dma((6,)),
             dma((views - 1,)), dma((views - 1,)), dma((views - 1,)), dma((views - 1,)),
         ],
         compiler_params=pltpu.CompilerParams(
-            collective_id=0, has_side_effects=True, vmem_limit_bytes=54 * 2**20
+            collective_id=0, has_side_effects=True, vmem_limit_bytes=44 * 2**20
         ),
         name="splat_step",
     )(seg_count, seg_block, ray_count, shift, gaussians, target)

time: 42.9 us -> 42 us (0.979)
  Pallas kernels: 37.8 us -> 36.2 us
  local copies, waits for them, and re-layouts: 2.94 us -> 3.58 us
    pallas_call x1, Pallas kernels: 37.8 us -> 36.2 us  [step(): pl.pallas_call(functools.partial(step_kernel, cells, views, slots, rows,...]
    unnamed x2 -> x10, local copies, waits for them, and re-layouts: 2.94 us -> 3.58 us
where the time goes in v2:
time: 42 us; the launch traced here: 41.7 us
  Pallas kernels  36.2 us (86%)
  local copies, waits for them, and re-layouts  3.58 us (9%)
  between operations  1.95 us (5%)
    pallas_call x1, Pallas kernels, step(): pl.pallas_call(functools.partial(step_kernel, cells, views, slots, rows,...  36.2 us
    unnamed x10, local copies, waits for them, and re-layouts  3.58 us

profile of v2, /device:TPU:0, one launch (start us, length us, event | category | flops | bytes accessed | tf_op | source)
XLA Modules:
  0.0 41.7 jit_solution(4779977167343852632)
XLA Ops:
  1.9 0.0 copy-start.2
  1.9 0.0 copy-start.3
  1.9 0.6 %copy-done.2 = s32[1,1,3]{2,1,0:T(1,128)S(1)} copy-done((s32[1,1,3]{2,1,0:T(1,128)S(1)}, s32[1,1,3]{2,1,0:T(1,128)}, u32[]{:S(2)}) %copy-start.2) | copy-done | bytes 36
  2.6 0.0 copy-done.3
  2.6 0.0 copy-start
  2.6 0.9 %copy-done = f32[16,9,256]{2,0,1:T(8,128)S(1)} copy-done((f32[16,9,256]{2,0,1:T(8,128)S(1)}, f32[16,9,256]{2,0,1:T(8,128)}, u32[]{:S(2)}) %copy-start) | copy-done | bytes 147480
  3.5 0.0 copy-start.1
  3.5 0.7 %copy-done.1 = f32[1,1,3,2304]{3,1,2,0:T(1,128)S(1)} copy-done((f32[1,1,3,2304]{3,1,2,0:T(1,128)S(1)}, f32[1,1,3,2304]{3,1,2,0:T(1,128)}, u32[]{:S(2)}) %copy-start.1) | copy-done | bytes 27672
  4.3 36.2 %splat_step.1 = (f32[144,256]{1,0:T(8,128)S(1)}, f32[3,1,2304]{2,1,0:T(1,128)S(1)}) custom-call(s32[1,1]{1,0:T(1,128)S(6)} %copy.11.count_ref, s32[1,1,3]{2,1,0:T(1,128)S(1)} %copy-done.2, s32[1,1]{1,0:T(1,128)S(6)} %copy.12.ray_ref, f32[1,2]{1,0:T(1,128)S(1)} %copy-done.3, f32[144,256]{1,0:T(8,128)S(1)} %bitcast.10, f32[3,1,2304]{2,1,0:T(1,128)S(1)} %bitcast.13), custom_call_target="tpu_custom_call" | custom-call | tf_op jit(solution)/shard_map/splat_step/pallas_call | solution.py:418
  40.5 0.6 %copy.13 = f32[1,1,3,2304]{3,1,2,0:T(1,128)} copy(f32[1,1,3,2304]{3,1,2,0:T(1,128)S(1)} %bitcast.12) | data formatting | bytes 55296
  41.1 0.7 %copy.14 = f32[16,9,256]{2,0,1:T(8,128)} copy(f32[16,9,256]{2,0,1:T(8,128)S(1)} %bitcast.11) | data formatting | bytes 294912
Async XLA Ops:
  1.9 0.7 %copy-start.2 = (s32[1,1,3]{2,1,0:T(1,128)S(1)}, s32[1,1,3]{2,1,0:T(1,128)}, u32[]{:S(2)}) copy-start(s32[1,1,3]{2,1,0:T(1,128)} %block_ref.1) | copy-start | bytes 40
  1.9 0.7 %copy-start.3 = (f32[1,2]{1,0:T(1,128)S(1)}, f32[1,2]{1,0:T(1,128)}, u32[]{:S(2)}) copy-start(f32[1,2]{1,0:T(1,128)} %shift_ref.1) | copy-start | bytes 28
  2.6 0.9 %copy-start = (f32[16,9,256]{2,0,1:T(8,128)S(1)}, f32[16,9,256]{2,0,1:T(8,128)}, u32[]{:S(2)}) copy-start(f32[16,9,256]{2,0,1:T(8,128)} %param.6) | copy-start | bytes 442372
  3.5 0.7 %copy-start.1 = (f32[1,1,3,2304]{3,1,2,0:T(1,128)S(1)}, f32[1,1,3,2304]{3,1,2,0:T(1,128)}, u32[]{:S(2)}) copy-start(f32[1,1,3,2304]{3,1,2,0:T(1,128)} %param.11) | copy-start | bytes 82948
